TPU v7x, 32 devices: a whole 2x2x4 slice. The times are simulated.
32 devices in a mesh: dp: 16 (over z, x, core), mp: 2 (over y).
Axes of the slice: x: 2, y: 2, z: 4, core: 2. Of those that a mesh axis runs over, the one named last changes fastest.
Arguments:
- inputs: bfloat16 [16384, 1024], P(('dp', 'mp')), may hold values from -6 to 6
- cotangent: bfloat16 [16384, 1024], P(('dp', 'mp')), may hold values from -6 to 6
- lengths: int32 [16], P('dp'), may hold values from 102 to 1024, as said below
- buckets: int32 [2047], replicated, may hold values from 0 to 31
- w_qkv: float32 [3, 1024, 1024], P(None, None, 'mp'), may hold values from -0.1875 to 0.1875
- w_out: float32 [1024, 1024], P(None, 'mp'), may hold values from -0.75 to 0.75
- w_ffn: float32 [2, 1024, 4096], P(None, None, 'mp'), may hold values from -0.1875 to 0.1875
- norm_params: float32 [4, 1024], replicated, may hold values from 0.5 to 1.5
- rel_bias: float32 [32, 16], replicated, may hold values from -5 to 5
- momentum_qkv: float32 [3, 1024, 1024], P(None, 'dp', 'mp'), may hold values from -1408 to 1408
- momentum_out: float32 [1024, 1024], P('dp', 'mp'), may hold values from -80 to 80
- momentum_ffn: float32 [2, 1024, 4096], P(None, 'dp', 'mp'), may hold values from -384 to 384
- momentum_norms: float32 [4, 1024], replicated, may hold values from -768 to 768
- momentum_bias: float32 [32, 16], replicated, may hold values from -224 to 224
- average_qkv: float32 [3, 1024, 1024], P(None, 'dp', 'mp'), may hold values from -0.1875 to 0.1875
- average_out: float32 [1024, 1024], P('dp', 'mp'), may hold values from -0.75 to 0.75
- average_ffn: float32 [2, 1024, 4096], P(None, 'dp', 'mp'), may hold values from -0.1875 to 0.1875
- average_norms: float32 [4, 1024], replicated, may hold values from 0.5 to 1.5
- average_bias: float32 [32, 16], replicated, may hold values from -5 to 5
Outputs:
- output: bfloat16 [16384, 1024], P(('dp', 'mp'))
- input_grad: float32 [16384, 1024], P(('dp', 'mp'))
- grad_qkv: float32 [3, 1024, 1024], P(None, 'dp', 'mp')
- next_moment_qkv: float32 [3, 1024, 1024], P(None, 'dp', 'mp')
- next_weight_qkv: float32 [3, 1024, 1024], P(None, 'dp', 'mp')
- next_average_qkv: float32 [3, 1024, 1024], P(None, 'dp', 'mp')
- grad_out: float32 [1024, 1024], P('dp', 'mp')
- next_moment_out: float32 [1024, 1024], P('dp', 'mp')
- next_weight_out: float32 [1024, 1024], P('dp', 'mp')
- next_average_out: float32 [1024, 1024], P('dp', 'mp')
- grad_ffn: float32 [2, 1024, 4096], P(None, 'dp', 'mp')
- next_moment_ffn: float32 [2, 1024, 4096], P(None, 'dp', 'mp')
- next_weight_ffn: float32 [2, 1024, 4096], P(None, 'dp', 'mp')
- next_average_ffn: float32 [2, 1024, 4096], P(None, 'dp', 'mp')
- grad_norms: float32 [4, 1024], replicated
- next_moment_norms: float32 [4, 1024], replicated
- next_weight_norms: float32 [4, 1024], replicated
- next_average_norms: float32 [4, 1024], replicated
- grad_bias: float32 [32, 16], replicated
- next_moment_bias: float32 [32, 16], replicated
- next_weight_bias: float32 [32, 16], replicated
- next_average_bias: float32 [32, 16], replicated
Inputs may be any that keep to these rules, and one draw needn't show every extreme that they name: `lengths`: each clip's number of valid frames; in every draw some clip has all 1024 valid.
All inputs are finite; a program needn't handle non-finite values.
Results may differ from a plain program's by a relative error of at most 0.017.
Values may be sent and summed in bfloat16 or wider, within the bound.
No kernel may reach another device: no remote copies, remote signals or barrier semaphores. Data moves between devices by JAX's collectives and lax.ppermute only.
A program may use at most 256 MiB of HBM per device.

v0:
```python
from functools import partial
import math

import jax
import jax.numpy as jnp
from jax import lax
from jax.sharding import PartitionSpec as P

HD = 64


highest = lax.Precision.HIGHEST
momentum_keep = 0.5
average_keep = 0.5


def normalize(values, gain_row, shift_row):
    row_mean = jnp.mean(values, axis=-1, keepdims=True)
    centered = values - row_mean
    spread = jnp.mean(centered * centered, axis=-1, keepdims=True)
    inverse = lax.rsqrt(spread + 1e-05)
    unit_rows = centered * inverse
    return (unit_rows * gain_row + shift_row, unit_rows, inverse)


def normalize_back(grad_normed, unit_rows, inverse, gain_row):
    grad_unit = grad_normed * gain_row
    first_mean = jnp.mean(grad_unit, axis=-1, keepdims=True)
    second_mean = jnp.mean(grad_unit * unit_rows, axis=-1, keepdims=True)
    grad_values = inverse * (grad_unit - first_mean - unit_rows * second_mean)
    return (grad_values, jnp.sum(grad_normed * unit_rows, axis=0), jnp.sum(grad_normed, axis=0))


def skew_start(seq_len, block_rows, first_row):
    return seq_len - block_rows - first_row


def skew_bias(bias_table, first_row, block_rows, seq_len):
    width = seq_len + block_rows - 1
    piece = lax.dynamic_slice_in_dim(
        bias_table, skew_start(seq_len, block_rows, first_row), width, 1
    )
    heads_local = piece.shape[0]
    tiled = jnp.tile(piece, (1, block_rows))
    tiled = tiled[:, block_rows - 1 : block_rows - 1 + block_rows * (width - 1)]
    return tiled.reshape(heads_local, block_rows, width - 1)[:, :, :seq_len]


def skew_grad(grad_block, block_rows, seq_len):
    width = seq_len + block_rows - 1
    heads_local = grad_block.shape[0]
    padded = jnp.pad(grad_block, ((0, 0), (0, 0), (0, width - 1 - seq_len)))
    flat = padded.reshape(heads_local, block_rows * (width - 1))
    flat = jnp.pad(flat, ((0, 0), (block_rows - 1, 1)))
    return jnp.sum(flat.reshape(heads_local, block_rows, width), axis=1)


def block_scores(query_block, keys_all, bias_table, first_row, key_valid, block_rows):
    seq_len = keys_all.shape[0]
    scores = (
        jnp.einsum("qhd,khd->hqk", query_block, keys_all, preferred_element_type=jnp.float32)
        * 0.125
    )
    scores = scores + skew_bias(bias_table, first_row, block_rows, seq_len)
    return jnp.where(key_valid[None, None, :], scores, -1000000000.0)


def clip_forward(queries, keys_all, values_all, key_valid, bias_table, block_rows):
    seq_len, heads_local, head_size = keys_all.shape

    def one_block(block_index):
        first_row = block_index * block_rows
        query_block = lax.dynamic_slice_in_dim(queries, first_row, block_rows, 0)
        scores = block_scores(query_block, keys_all, bias_table, first_row, key_valid, block_rows)
        row_top = jnp.max(scores, axis=-1, keepdims=True)
        raised = jnp.exp(scores - row_top)
        totals = jnp.sum(raised, axis=-1, keepdims=True)
        soft_weights = (raised / totals).astype(jnp.bfloat16)
        context = jnp.einsum(
            "hqk,khd->qhd", soft_weights, values_all, preferred_element_type=jnp.float32
        ).astype(jnp.bfloat16)
        return (context, (row_top + jnp.log(totals))[..., 0])

    context, log_totals = lax.map(one_block, jnp.arange(seq_len // block_rows, dtype=jnp.int32))
    return (context.reshape(seq_len, heads_local, head_size), log_totals)


def clip_backward(
    queries, keys_all, values_all, context_grad, log_totals, key_valid, bias_table, block_rows
):
    seq_len, heads_local, head_size = keys_all.shape
    width = seq_len + block_rows - 1

    def one_block(running, block_index):
        key_grad, value_grad, offset_grad = running
        first_row = block_index * block_rows
        query_block = lax.dynamic_slice_in_dim(queries, first_row, block_rows, 0)
        grad_block = lax.dynamic_slice_in_dim(context_grad, first_row, block_rows, 0)
        scores = block_scores(query_block, keys_all, bias_table, first_row, key_valid, block_rows)
        soft_full = jnp.exp(scores - log_totals[block_index][..., None])
        prob_grad = jnp.einsum(
            "qhd,khd->hqk", grad_block, values_all, preferred_element_type=jnp.float32
        )
        row_dot = jnp.sum(soft_full * prob_grad, axis=-1, keepdims=True)
        score_grad = (soft_full * (prob_grad - row_dot)).astype(jnp.bfloat16)
        query_grad = (
            jnp.einsum("hqk,khd->qhd", score_grad, keys_all, preferred_element_type=jnp.float32)
            * 0.125
        ).astype(jnp.bfloat16)
        key_grad = (
            key_grad
            + jnp.einsum(
                "hqk,qhd->khd", score_grad, query_block, preferred_element_type=jnp.float32
            )
            * 0.125
        )
        value_grad = value_grad + jnp.einsum(
            "hqk,qhd->khd",
            soft_full.astype(jnp.bfloat16),
            grad_block,
            preferred_element_type=jnp.float32,
        )
        diagonal_sums = skew_grad(score_grad.astype(jnp.float32), block_rows, seq_len)
        start = skew_start(seq_len, block_rows, first_row)
        current = lax.dynamic_slice_in_dim(offset_grad, start, width, 1)
        offset_grad = lax.dynamic_update_slice_in_dim(
            offset_grad, current + diagonal_sums, start, 1
        )
        return ((key_grad, value_grad, offset_grad), query_grad)

    start_state = (
        jnp.zeros((seq_len, heads_local, head_size), jnp.float32),
        jnp.zeros((seq_len, heads_local, head_size), jnp.float32),
        jnp.zeros((heads_local, 2 * seq_len - 1), jnp.float32),
    )
    (key_grad, value_grad, offset_grad), query_grads = lax.scan(
        one_block, start_state, jnp.arange(seq_len // block_rows, dtype=jnp.int32)
    )
    return (
        query_grads.reshape(seq_len, heads_local, head_size),
        key_grad.astype(jnp.bfloat16),
        value_grad.astype(jnp.bfloat16),
        offset_grad,
    )


def apply_update(weight, momentum, average, gradient, step_rate):
    next_moment = momentum_keep * momentum + gradient
    next_weight = weight - step_rate * (gradient + momentum_keep * next_moment)
    next_average = average_keep * average + (1.0 - average_keep) * next_weight
    return (next_moment, next_weight, next_average)


def per_device(
    inputs,
    cotangent,
    lengths,
    buckets,
    w_qkv,
    w_out,
    w_ffn,
    norm_params,
    rel_bias,
    momentum_qkv,
    momentum_out,
    momentum_ffn,
    momentum_norms,
    momentum_bias,
    average_qkv,
    average_out,
    average_ffn,
    average_norms,
    average_bias,
):
    model_size = lax.axis_size("mp")
    data_size = lax.axis_size("dp")
    rows_local = inputs.shape[0]
    clip_count = lengths.shape[0]
    all_rows = rows_local * model_size
    seq_len = all_rows // clip_count
    width_local = w_qkv.shape[2]
    heads_local = width_local // HD
    block_rows = seq_len // 2
    head_first = lax.axis_index("mp") * heads_local
    data_index = lax.axis_index("dp")
    share_rows = momentum_out.shape[0]
    inputs_wide = inputs.astype(jnp.float32)
    normed_one, unit_one, inverse_one = normalize(inputs_wide, norm_params[0], norm_params[1])
    gathered_one = lax.all_gather(normed_one.astype(jnp.bfloat16), "mp", axis=0, tiled=True)
    weights_qkv = w_qkv.astype(jnp.bfloat16)
    projected = jnp.einsum(
        "sd,tdc->tsc", gathered_one, weights_qkv, preferred_element_type=jnp.float32
    ).astype(jnp.bfloat16)
    bias_local = lax.dynamic_slice_in_dim(rel_bias, head_first, heads_local, 1)
    bucket_hits = (
        buckets[:, None] == jnp.arange(rel_bias.shape[0], dtype=jnp.int32)[None, :]
    ).astype(jnp.float32)
    bias_table = jnp.dot(bucket_hits, bias_local, precision=highest).T
    shaped = projected.reshape(3, clip_count, seq_len, heads_local, HD)
    clip_index = 0
    key_valid = jnp.arange(seq_len, dtype=jnp.int32) < lengths[clip_index]
    context, log_totals = clip_forward(
        shaped[0, clip_index],
        shaped[1, clip_index],
        shaped[2, clip_index],
        key_valid,
        bias_table,
        block_rows,
    )
    log_list = [log_totals]
    valid_list = [key_valid]
    context_all = context.reshape(all_rows, width_local)
    weights_out = w_out.astype(jnp.bfloat16)
    row_piece = context_all
    branch = lax.psum_scatter(
        jnp.einsum("sc,dc->sd", row_piece, weights_out, preferred_element_type=jnp.float32),
        "mp",
        scatter_dimension=0,
        tiled=True,
    )
    middle = inputs_wide + branch
    normed_two, unit_two, inverse_two = normalize(middle, norm_params[2], norm_params[3])
    gathered_two = lax.all_gather(normed_two.astype(jnp.bfloat16), "mp", axis=0, tiled=True)
    weights_ffn = w_ffn.astype(jnp.bfloat16)
    hidden_pre = jnp.dot(gathered_two, weights_ffn[0], preferred_element_type=jnp.float32)
    hidden, gelu_back = jax.vjp(partial(jax.nn.gelu, approximate=False), hidden_pre)
    hidden = hidden.astype(jnp.bfloat16)
    row_piece = lax.slice_in_dim(hidden, 0, rows_local * lax.axis_size("mp"), axis=0)
    output = (
        middle
        + lax.psum_scatter(
            jnp.einsum(
                "sf,df->sd", row_piece, weights_ffn[1], preferred_element_type=jnp.float32
            ).astype(jnp.bfloat16),
            "mp",
            scatter_dimension=0,
            tiled=True,
        ).astype(jnp.float32)
    ).astype(jnp.bfloat16)
    gathered_cot = lax.all_gather(cotangent, "mp", axis=0, tiled=True)
    down_grad = jnp.einsum("sd,sf->df", gathered_cot, hidden, preferred_element_type=jnp.float32)
    hidden_grad = jnp.dot(gathered_cot, weights_ffn[1], preferred_element_type=jnp.float32)
    pre_grad = gelu_back(hidden_grad)[0].astype(jnp.bfloat16)
    up_grad = jnp.einsum("sd,sf->df", gathered_two, pre_grad, preferred_element_type=jnp.float32)
    ffn_grad = jnp.stack([up_grad, down_grad])
    ffn_total = lax.psum(ffn_grad.astype(jnp.bfloat16), "dp").astype(jnp.float32)
    ffn_share = lax.dynamic_slice_in_dim(ffn_total, data_index * share_rows, share_rows, 1)
    row_piece = pre_grad
    normed_two_grad = lax.psum_scatter(
        jnp.einsum("sf,df->sd", row_piece, weights_ffn[0], preferred_element_type=jnp.float32),
        "mp",
        scatter_dimension=0,
        tiled=True,
    )
    middle_back, gain_two_grad, shift_two_grad = normalize_back(
        normed_two_grad, unit_two, inverse_two, norm_params[2]
    )
    middle_grad = cotangent.astype(jnp.float32) + middle_back
    gathered_branch = lax.all_gather(middle_grad.astype(jnp.bfloat16), "mp", axis=0, tiled=True)
    out_grad = jnp.einsum(
        "sd,sc->dc", gathered_branch, context_all, preferred_element_type=jnp.float32
    )
    context_grad = jnp.dot(gathered_branch, weights_out, preferred_element_type=jnp.float32).astype(
        jnp.bfloat16
    )
    context_grad = context_grad.reshape(clip_count, seq_len, heads_local, HD)
    clip_index = 0
    query_grad, key_grad, value_grad, offset_grad = clip_backward(
        shaped[0, clip_index],
        shaped[1, clip_index],
        shaped[2, clip_index],
        context_grad[clip_index],
        log_list[clip_index],
        valid_list[clip_index],
        bias_table,
        block_rows,
    )
    grad_parts = jnp.stack([query_grad, key_grad, value_grad]).reshape(3, seq_len, width_local)
    qkv_weight_grad = jnp.einsum(
        "sd,tsc->tdc", gathered_one, grad_parts, preferred_element_type=jnp.float32
    )
    qkv_total, out_total = (
        lax.psum(qkv_weight_grad.astype(jnp.bfloat16), "dp").astype(jnp.float32),
        lax.psum(out_grad[None].astype(jnp.bfloat16), "dp").astype(jnp.float32),
    )
    qkv_share = lax.dynamic_slice_in_dim(qkv_total, data_index * share_rows, share_rows, 1)
    out_share = lax.dynamic_slice_in_dim(out_total, data_index * share_rows, share_rows, 1)[0]
    row_piece = grad_parts
    normed_one_grad = lax.psum_scatter(
        jnp.einsum(
            "tsc,tdc->sd", row_piece, weights_qkv, preferred_element_type=jnp.float32
        ).astype(jnp.bfloat16),
        "mp",
        scatter_dimension=0,
        tiled=True,
    ).astype(jnp.float32)
    input_back, gain_one_grad, shift_one_grad = normalize_back(
        normed_one_grad, unit_one, inverse_one, norm_params[0]
    )
    input_grad = middle_grad + input_back
    bias_grad_local = jnp.einsum("rb,hr->bh", bucket_hits, offset_grad, precision=highest)
    bias_grad_full = lax.dynamic_update_slice_in_dim(
        jnp.zeros(rel_bias.shape, jnp.float32), bias_grad_local, head_first, 1
    )
    norm_grad_local = jnp.stack([gain_one_grad, shift_one_grad, gain_two_grad, shift_two_grad])
    norm_grad, bias_grad = lax.psum((norm_grad_local, bias_grad_full), ("dp", "mp"))
    scale_factor = 1.0 / math.sqrt(float(all_rows * data_size))
    weight_qkv_share = lax.dynamic_slice_in_dim(w_qkv, data_index * share_rows, share_rows, 1)
    weight_out_share = lax.dynamic_slice_in_dim(w_out, data_index * share_rows, share_rows, 0)
    weight_ffn_share = lax.dynamic_slice_in_dim(w_ffn, data_index * share_rows, share_rows, 1)
    moment_qkv, weight_qkv, mean_qkv = apply_update(
        weight_qkv_share, momentum_qkv, average_qkv, qkv_share, 0.3 * scale_factor
    )
    moment_out, weight_out, mean_out = apply_update(
        weight_out_share, momentum_out, average_out, out_share, 0.1 * scale_factor
    )
    moment_ffn, weight_ffn, mean_ffn = apply_update(
        weight_ffn_share, momentum_ffn, average_ffn, ffn_share, 0.05 * scale_factor
    )
    moment_norms, weight_norms, mean_norms = apply_update(
        norm_params, momentum_norms, average_norms, norm_grad, 0.05 * scale_factor
    )
    moment_bias, weight_bias, mean_bias = apply_update(
        rel_bias, momentum_bias, average_bias, bias_grad, 0.05 * scale_factor
    )
    return (
        output,
        input_grad,
        qkv_share,
        moment_qkv,
        weight_qkv,
        mean_qkv,
        out_share,
        moment_out,
        weight_out,
        mean_out,
        ffn_share,
        moment_ffn,
        weight_ffn,
        mean_ffn,
        norm_grad,
        moment_norms,
        weight_norms,
        mean_norms,
        bias_grad,
        moment_bias,
        weight_bias,
        mean_bias,
    )


def solution(mesh):
    return jax.shard_map(
        per_device,
        mesh=mesh,
        in_specs=(
            P(("dp", "mp"), None),
            P(("dp", "mp"), None),
            P("dp"),
            P(),
            P(None, None, "mp"),
            P(None, "mp"),
            P(None, None, "mp"),
            P(),
            P(),
            P(None, "dp", "mp"),
            P("dp", "mp"),
            P(None, "dp", "mp"),
            P(),
            P(),
            P(None, "dp", "mp"),
            P("dp", "mp"),
            P(None, "dp", "mp"),
            P(),
            P(),
        ),
        out_specs=(
            P(("dp", "mp"), None),
            P(("dp", "mp"), None),
            P(None, "dp", "mp"),
            P(None, "dp", "mp"),
            P(None, "dp", "mp"),
            P(None, "dp", "mp"),
            P("dp", "mp"),
            P("dp", "mp"),
            P("dp", "mp"),
            P("dp", "mp"),
            P(None, "dp", "mp"),
            P(None, "dp", "mp"),
            P(None, "dp", "mp"),
            P(None, "dp", "mp"),
            P(),
            P(),
            P(),
            P(),
            P(),
            P(),
            P(),
            P(),
        ),
        check_vma=False,
    )
```

profile of v0, /device:TPU:0, one launch (start us, length us, event | category | flops | bytes accessed | tf_op | source)
XLA Modules:
  0.0 1635.0 jit_solution(17605507637681976269)
XLA Ops:
  16.6 34.5 %all-gather.5.cloned.1.call-done = bf16[1024,1024]{1,0:T(8,128)(2,1)} async-done(((bf16[512,1024]{1,0:T(8,128)(2,1)}), bf16[1024,1024]{1,0:T(8,128)(2,1)}) %all-gather.5.cloned.1.call-update) | async-done | bytes 2097168 | tf_op jit(solution)/shard_map/all_gather | solution.py:189
  60.7 316.4 %while.34 = (s32[]{:T(128)}, bf16[2,512,8,64]{1,3,2,0:T(8,128)(2,1)}, f32[2,8,512]{2,1,0:T(8,128)}, s32[2]{0:T(128)S(1)}, bf16[1024,8,64]{0,2,1:T(8,128)(2,1)}, ...) while((s32[]{:T(128)}, ...), condition=%wide.region_5.6_spmd.clone, body=%wide.region_2.5_spmd.clone.sunk | while | flops 1111749632 | bytes 359729408 | solution.py:84
  75.2 37.7 %reshape.205 = f32[6287360]{0:T(1024)} reshape(f32[8,512,1535]{2,1,0:T(8,128)} %tile.32) | data formatting | bytes 50298880 | tf_op jit(solution)/shard_map/while
  112.9 23.9 %tile.33 = f32[8,785920]{1,0:T(8,128)} reshape(f32[6287360]{0:T(1024)} %reshape.205) | data formatting | bytes 50298880 | tf_op jit(solution)/shard_map/while/body/eval_jaxpr/tile | solution.py:44
  176.3 24.1 %reshape.207 = f32[8,512,1534]{2,1,0:T(8,128)} reshape(f32[6283264]{0:T(1024)} %reshape.206) | data formatting | bytes 50266112 | tf_op jit(solution)/shard_map/while/body/eval_jaxpr/reshape | solution.py:46
  233.1 37.7 %reshape.205 = f32[6287360]{0:T(1024)} reshape(f32[8,512,1535]{2,1,0:T(8,128)} %tile.32) | data formatting | bytes 50298880 | tf_op jit(solution)/shard_map/while
  270.8 23.9 %tile.33 = f32[8,785920]{1,0:T(8,128)} reshape(f32[6287360]{0:T(1024)} %reshape.205) | data formatting | bytes 50298880 | tf_op jit(solution)/shard_map/while/body/eval_jaxpr/tile | solution.py:44
  334.2 24.1 %reshape.207 = f32[8,512,1534]{2,1,0:T(8,128)} reshape(f32[6283264]{0:T(1024)} %reshape.206) | data formatting | bytes 50266112 | tf_op jit(solution)/shard_map/while/body/eval_jaxpr/reshape | solution.py:46
  384.2 54.4 %reduce-scatter.5.cloned.1.call-done = f32[512,1024]{1,0:T(8,128)} async-done(((f32[1024,1024]{1,0:T(8,128)}), f32[512,1024]{1,0:T(8,128)}) %reduce-scatter.5.cloned.1.call-update) | async-done | bytes 2097168 | tf_op jit(solution)/shard_map/reduce_scatter | solution.py:215
  475.8 26.0 %multiply_convert_fusion.1 = (bf16[1024,2048]{1,0:T(8,128)(2,1)}, f32[1024,2048]{1,0:T(8,128)}, f32[1024,2048]{1,0:T(8,128)}) fusion(bf16[1024,1024]{1,0:T(8,128)(2,1)} %all-gather.7.cloned.1.call-done, bf16[2,1024,2048]{2,1,0:T(8,128)(2,1)} %convert_element_type.136), kind=kOutput, calls=%fused_computation.48 | convolution fusion | flops 4431282176 | bytes 27262976 | tf_op jit(solution)/shard_map/dot_general | solution.py:225
  540.9 44.9 %reduce-scatter.9.cloned.1.call-done = f32[512,1024]{1,0:T(8,128)} async-done(((f32[1024,1024]{1,0:T(8,128)}), f32[512,1024]{1,0:T(8,128)}) %reduce-scatter.9.cloned.1.call-update) | async-done | bytes 2097168 | tf_op jit(solution)/shard_map/reduce_scatter | solution.py:249
  588.8 31.5 %reduce-scatter.7.cloned.1.call-done = bf16[512,1024]{1,0:T(8,128)(2,1)} async-done(((bf16[1024,1024]{1,0:T(8,128)(2,1)}), bf16[512,1024]{1,0:T(8,128)(2,1)}) %reduce-scatter.7.cloned.1.call-update) | async-done | bytes 1048592 | tf_op jit(solution)/shard_map/reduce_scatter | solution.py:231
  625.5 33.2 %all-gather.11.cloned.1.call-done = bf16[1024,1024]{1,0:T(8,128)(2,1)} async-done(((bf16[512,1024]{1,0:T(8,128)(2,1)}), bf16[1024,1024]{1,0:T(8,128)(2,1)}) %all-gather.11.cloned.1.call-update) | async-done | bytes 2097168 | tf_op jit(solution)/shard_map/all_gather | solution.py:259
  664.5 658.4 %while.35 = (s32[]{:T(128)}, f32[1024,8,64]{0,2,1:T(8,128)}, f32[1024,8,64]{0,2,1:T(8,128)}, f32[8,2047]{1,0:T(8,128)}, bf16[2,512,8,64]{1,3,2,0:T(8,128)(2,1)},...) while((s32[]{:T(128)}, f32[1024,8,64]{0,2,1:T(8,128)}, ...), condition=%wide.region_16.17_spmd.clone, body=%wide.region_13.16_spmd.clone.sunk | while | flops 2742014976 | bytes 761317440 | solution.py:136
  690.5 37.8 %reshape.209 = f32[6287360]{0:T(1024)} reshape(f32[8,512,1535]{2,1,0:T(8,128)} %tile.34) | data formatting | bytes 50298880 | tf_op jit(solution)/shard_map/while
  728.3 23.8 %tile.35 = f32[8,785920]{1,0:T(8,128)} reshape(f32[6287360]{0:T(1024)} %reshape.209) | data formatting | bytes 50298880 | tf_op jit(solution)/shard_map/while/body/eval_jaxpr/tile | solution.py:44
  792.0 24.1 %reshape.211 = f32[8,512,1534]{2,1,0:T(8,128)} reshape(f32[6283264]{0:T(1024)} %reshape.210) | data formatting | bytes 50266112 | tf_op jit(solution)/shard_map/while/body/eval_jaxpr/reshape | solution.py:46
  938.2 39.2 %reshape.215 = f32[8,512,1535]{2,1,0:T(8,128)} reshape(f32[6287360]{0:T(1024)} %reshape.214) | data formatting | bytes 50298880 | tf_op jit(solution)/shard_map/while/body/eval_jaxpr/reshape | solution.py:55
  1014.9 38.0 %reshape.209 = f32[6287360]{0:T(1024)} reshape(f32[8,512,1535]{2,1,0:T(8,128)} %tile.34) | data formatting | bytes 50298880 | tf_op jit(solution)/shard_map/while
  1052.9 23.8 %tile.35 = f32[8,785920]{1,0:T(8,128)} reshape(f32[6287360]{0:T(1024)} %reshape.209) | data formatting | bytes 50298880 | tf_op jit(solution)/shard_map/while/body/eval_jaxpr/tile | solution.py:44
  1116.3 24.1 %reshape.211 = f32[8,512,1534]{2,1,0:T(8,128)} reshape(f32[6283264]{0:T(1024)} %reshape.210) | data formatting | bytes 50266112 | tf_op jit(solution)/shard_map/while/body/eval_jaxpr/reshape | solution.py:46
  1265.0 39.2 %reshape.215 = f32[8,512,1535]{2,1,0:T(8,128)} reshape(f32[6287360]{0:T(1024)} %reshape.214) | data formatting | bytes 50298880 | tf_op jit(solution)/shard_map/while/body/eval_jaxpr/reshape | solution.py:55
  1383.3 41.4 %all-reduce.2 = (f32[4,1024]{1,0:T(4,128)S(1)}, f32[32,16]{0,1:T(8,128)S(1)}) all-reduce(f32[4,1024]{1,0:T(4,128)S(1)} %pad_maximum_fusion.4, f32[32,16]{0,1:T(8,128)S(1)} %convolution_dynamic-update-slice_fusion), channel_id=1, replica_groups=mesh['dp'=16,'mp'=2] {'dp','mp'}, use_global_device_ids=true, to_apply=%region_27.28 | all-reduce | flops 4608 | bytes 36864 | tf_op jit(solution)/shard_map/psum | solution.py:306
  1429.3 185.8 %all-reduce.6.cloned.1.call-done = (bf16[3,1024,512]{1,2,0:T(8,128)(2,1)}, bf16[1,1024,512]{2,1,0:T(8,128)(2,1)}, bf16[2,1024,2048]{2,1,0:T(8,128)(2,1)}) async-done(((bf16[3,1024,512]{1,2,0:T(8,128)(2,1)}, bf16[1,1024,512]{2,1,0:T(8,128)(2,1)}, bf16[2,1024,2048]{2,1,0:T(8,128)(2,1)}), (bf16[3,1024,512]{1,2,0:T(8,128)(2,1)}, bf16[1,1024,512]{2,1,0:T(8,128)(2,1)}, ...) | async-done | bytes 12582928 | tf_op jit(solution)/shard_map/psum | solution.py:283
  (277 shorter events, 732.1 us)
Async XLA Ops:
  7.2 43.9 %all-gather.5.cloned.1.call-start = ((), (), s32[]{:S(2)}) async-start(), calls=%async_computation.4 | async-start | bytes 3145728 | tf_op jit(solution)/shard_map/all_gather | solution.py:189
  15.1 423.5 %reduce-scatter.5.cloned.1.call-start = ((), (), s32[]{:S(2)}) async-start(), calls=%async_computation.5 | async-start | bytes 6291456 | tf_op jit(solution)/shard_map/reduce_scatter | solution.py:215
  384.1 57.0 %copy-start.27 = (f32[1,1024]{1,0:T(1,128)S(1)}, f32[1,1024]{1,0:T(1,128)}, u32[]{:S(2)}) copy-start(f32[1,1024]{1,0:T(1,128)} %get-tuple-element.505) | copy-start | bytes 12292
  384.1 56.9 %copy-start.37 = (f32[1,1024]{1,0:T(1,128)S(1)}, f32[1,1024]{1,0:T(1,128)}, u32[]{:S(2)}) copy-start(f32[1,1024]{1,0:T(1,128)} %get-tuple-element.508) | copy-start | bytes 12292
  384.2 91.6 %all-gather.7.cloned.1.call-start = ((), (), s32[]{:S(2)}) async-start(), calls=%async_computation.6 | async-start | bytes 3145728 | tf_op jit(solution)/shard_map/all_gather | solution.py:223
  442.5 67.9 %all-gather.9.cloned.1.call-start = ((), (), s32[]{:S(2)}) async-start(), calls=%async_computation.8 | async-start | bytes 3145728 | tf_op jit(solution)/shard_map/all_gather | solution.py:240
  443.1 142.7 %reduce-scatter.9.cloned.1.call-start = ((), (), s32[]{:S(2)}) async-start(), calls=%async_computation.9 | async-start | bytes 6291456 | tf_op jit(solution)/shard_map/reduce_scatter | solution.py:249
  531.3 89.0 %reduce-scatter.7.cloned.1.call-start = ((), (), s32[]{:S(2)}) async-start(), calls=%async_computation.7 | async-start | bytes 3145728 | tf_op jit(solution)/shard_map/reduce_scatter | solution.py:231
  540.9 117.9 %all-gather.11.cloned.1.call-start = ((), (), s32[]{:S(2)}) async-start(), calls=%async_computation.10 | async-start | bytes 3145728 | tf_op jit(solution)/shard_map/all_gather | solution.py:259
  625.5 755.5 %reduce-scatter.11.cloned.1.call-start = ((), (), s32[]{:S(2)}) async-start(), calls=%async_computation.11 | async-start | bytes 3145728 | tf_op jit(solution)/shard_map/reduce_scatter | solution.py:289
  664.7 151.4 %copy-start.1 = (bf16[1024,8,64]{0,2,1:T(8,128)(2,1)}, bf16[1024,8,64]{0,2,1:T(8,128)(2,1)S(1)}, u32[]{:S(2)}) copy-start(bf16[1024,8,64]{0,2,1:T(8,128)(2,1)S(1)} %get-tuple-element.748) | copy-start | bytes 3145732 | tf_op jit(solution)/shard_map/while
  989.1 151.3 %copy-start.1 = (bf16[1024,8,64]{0,2,1:T(8,128)(2,1)}, bf16[1024,8,64]{0,2,1:T(8,128)(2,1)S(1)}, u32[]{:S(2)}) copy-start(bf16[1024,8,64]{0,2,1:T(8,128)(2,1)S(1)} %get-tuple-element.748) | copy-start | bytes 3145732 | tf_op jit(solution)/shard_map/while
  1343.0 272.1 %all-reduce.6.cloned.1.call-start = ((), (), s32[]{:S(2)}) async-start(), calls=%async_computation.12 | async-start | bytes 25165824 | tf_op jit(solution)/shard_map/psum | solution.py:283
  1372.7 52.6 %copy-start.28 = (f32[4,1024]{1,0:T(4,128)S(1)}, f32[4,1024]{1,0:T(4,128)}, u32[]{:S(2)}) copy-start(f32[4,1024]{1,0:T(4,128)} %param.30) | copy-start | bytes 49156
  1372.7 53.3 %copy-start.12 = (f32[512,1024]{1,0:T(8,128)S(1)}, f32[512,1024]{1,0:T(8,128)}, u32[]{:S(2)}) copy-start(f32[512,1024]{1,0:T(8,128)} %get-tuple-element.492) | copy-start | bytes 6291460
  1375.0 49.6 %copy-start.43 = (f32[32,16]{0,1:T(8,128)S(1)}, f32[32,16]{0,1:T(8,128)}, u32[]{:S(2)}) copy-start(f32[32,16]{0,1:T(8,128)} %param.41) | copy-start | bytes 6148
  1375.0 49.6 %copy-start.44 = (f32[32,16]{0,1:T(8,128)S(1)}, f32[32,16]{0,1:T(8,128)}, u32[]{:S(2)}) copy-start(f32[32,16]{0,1:T(8,128)} %param.36) | copy-start | bytes 6148
  1375.1 50.3 %copy-start.38 = (f32[4,1024]{1,0:T(4,128)S(1)}, f32[4,1024]{1,0:T(4,128)}, u32[]{:S(2)}) copy-start(f32[4,1024]{1,0:T(4,128)} %param.40) | copy-start | bytes 49156
  1375.1 50.2 %copy-start.39 = (f32[4,1024]{1,0:T(4,128)S(1)}, f32[4,1024]{1,0:T(4,128)}, u32[]{:S(2)}) copy-start(f32[4,1024]{1,0:T(4,128)} %param.35) | copy-start | bytes 49156
  1375.1 50.9 %copy-start.30 = (f32[1,1024]{1,0:T(1,128)S(1)}, f32[1,1024]{1,0:T(1,128)}, u32[]{:S(2)}) copy-start(f32[1,1024]{1,0:T(1,128)} %copy-done.29) | copy-start | bytes 12292
  1375.1 50.9 %copy-start.32 = (f32[512]{0:T(512)S(1)}, f32[512]{0:T(512)}, u32[]{:S(2)}) copy-start(f32[512]{0:T(512)} %copy-done.31) | copy-start | bytes 6148
  1375.1 50.9 %copy-start.34 = (f32[512]{0:T(512)S(1)}, f32[512]{0:T(512)}, u32[]{:S(2)}) copy-start(f32[512]{0:T(512)} %copy-done.33) | copy-start | bytes 6148
  1424.6 191.7 %copy-start.40 = (f32[4,1024]{1,0:T(4,128)}, f32[4,1024]{1,0:T(4,128)S(1)}, u32[]{:S(2)}) copy-start(f32[4,1024]{1,0:T(4,128)S(1)} %get-tuple-element.469) | copy-start | bytes 49156
  1424.6 191.7 %copy-start.45 = (f32[32,16]{0,1:T(8,128)}, f32[32,16]{0,1:T(8,128)S(1)}, u32[]{:S(2)}) copy-start(f32[32,16]{0,1:T(8,128)S(1)} %get-tuple-element.470) | copy-start | bytes 6148
  (49 other events, 410.9 us)
Sparse Core Ops, SparseCore 0:
  15.2 35.8 all-gather.4
  384.2 54.2 reduce-scatter.4
  442.6 33.1 all-gather.6
  477.2 33.1 all-gather.8
  531.4 54.3 reduce-scatter.8
  588.5 31.8 reduce-scatter.6
  625.6 33.1 all-gather.10
  1343.1 31.8 reduce-scatter.10
  1380.0 235.0 all-reduce.5
where the time goes:
time: 1650 us; the launch traced here: 1630 us
  local copies, waits for them, and re-layouts  800 us (48%)
  waiting for transfers between devices  416 us (25%)
  matrix products  209 us (13%)
  other arithmetic  138 us (8%)
  blocking collectives  41.4 us (3%)
    while x64, local copies, waits for them, and re-layouts  321 us
    psum x1, waiting for transfers between devices, per_device(): lax.psum(qkv_weight_grad.astype(jnp.bfloat16), 'dp').astype(jnp.float32)  186 us
    another operation x8, local copies, waits for them, and re-layouts, skew_bias(): tiled = jnp.tile(piece, (1, block_rows))  142 us
    reshape x4, local copies, waits for them, and re-layouts, skew_bias(): return tiled.reshape(heads_local, block_rows, width - 1)[:, :, :seq_len]  96.5 us
    reshape x2, local copies, waits for them, and re-layouts, skew_grad(): return jnp.sum(flat.reshape(heads_local, block_rows, width), axis=1)  78.4 us
    slice x4, local copies, waits for them, and re-layouts, skew_bias(): tiled = tiled[:, block_rows - 1:block_rows - 1 + block_rows * (width - 1)]  77.9 us
    dot_general x4, matrix products, block_scores(): jnp.einsum('qhd,khd->hqk', query_block, keys_all, preferred_element_type=...  56 us
    reduce_scatter x1, waiting for transfers between devices, per_device(): lax.psum_scatter(jnp.einsum('sc,dc->sd', row_piece, weights_out, preferre...  54.4 us
  transfers between devices with their start and end apart: 9, of which 8 were waited for; matrix products, arithmetic and copies ran while one was open for 6% of the time, Pallas kernels for 0%

commit v1 on v0

v1 whole, which is shorter than its diff:
```python
import math

import jax
import jax.numpy as jnp
from jax import lax
from jax.experimental import pallas as pl
from jax.experimental.pallas import tpu as pltpu
from jax.sharding import PartitionSpec as P

HD = 64
PAIR = 2 * HD
QB = 128
f32 = jnp.float32
bf16 = jnp.bfloat16
ROWS_BY_ROWS = (((1,), (1,)), ((), ()))
COLS_BY_COLS = (((0,), (0,)), ((), ()))
VMEM_LIMIT = 56 * 2**20

highest = lax.Precision.HIGHEST
momentum_keep = 0.5
average_keep = 0.5


def skew_kernel(tab_ref, rev_ref, fwd_ref, bwd_ref):
    width = tab_ref.shape[2]
    for src, dst in ((tab_ref, fwd_ref), (rev_ref, bwd_ref)):
        rows = jnp.broadcast_to(src[0], (QB, width))
        rolled = pltpu.roll(rows, width - (QB - 1), 1, stride=1, stride_axis=0)
        dst[0] = rolled[:, : width - QB]

def skew_tables(table):
    heads, width = table.shape
    pad = jnp.pad(table, ((0,0),(0,1)))[:, None, :]
    rev = jnp.pad(table[:, ::-1], ((0,0),(0,1)))[:, None, :]
    width += 1
    spec = pl.BlockSpec((1,1,width), lambda h:(h,0,0))
    ospec = pl.BlockSpec((1,QB,width-QB), lambda h:(h,0,0))
    o = jax.ShapeDtypeStruct((heads,QB,width-QB), f32)
    return pl.pallas_call(skew_kernel, grid=(heads,), in_specs=[spec,spec], out_specs=[ospec,ospec], out_shape=[o,o], name="skew")(pad, rev)

def split3(x):
    a = x.astype(bf16).astype(f32)
    r = x - a
    b = r.astype(bf16).astype(f32)
    return a, b, r - b

def key_side(k, valid_row, own, lane, first):
    extra = jnp.where(lane == first, valid_row, jnp.where((lane > first) & (lane < first + 4), 1.0, 0.0))
    return jnp.where(own, k, extra).astype(bf16)

def fwd_kernel(len_ref, q_ref, k_ref, v_ref, t_ref, o_ref, lse_ref, kx_ref, vx_ref):
    L = k_ref.shape[0]; R = q_ref.shape[0]
    lane = lax.broadcasted_iota(jnp.int32, (L, PAIR), 1)
    row = lax.broadcasted_iota(jnp.int32, (L, PAIR), 0)
    mask = jnp.where(row < len_ref[0], 0.0, -1e9)
    k = k_ref[...].astype(f32); v = v_ref[...].astype(f32)
    for h in range(2):
        own = (lane >= HD) if h else (lane < HD)
        kx_ref[h] = key_side(k, mask, own, lane, 0 if h else HD)
        vx_ref[h] = jnp.where(own, v, 1.0).astype(bf16)
    lq = lax.broadcasted_iota(jnp.int32, (QB, PAIR), 1)
    def body(a, _):
        rows = pl.ds(pl.multiple_of(a*QB, QB), QB)
        q = q_ref[rows, :].astype(f32) * 0.125
        start = pl.multiple_of(L - QB - a*QB, QB)
        outs=[]; ls=[]
        for h in range(2):
            own = (lq >= HD) if h else (lq < HD)
            first = 0 if h else HD
            qx = jnp.where(own, q, jnp.where(lq == first, 1.0, 0.0)).astype(bf16)
            s = lax.dot_general(qx, kx_ref[h], ROWS_BY_ROWS, preferred_element_type=f32)
            s = s + t_ref[h, :, pl.ds(start, L)]
            m = jnp.max(s, axis=1, keepdims=True)
            e = jnp.exp(s - m).astype(bf16)
            pv = jnp.dot(e, vx_ref[h], preferred_element_type=f32)
            tot = pv[:, :1] if h else pv[:, HD:HD+1]
            outs.append(pv / tot)
            ls.append(m + jnp.log(tot))
        o_ref[rows, :] = jnp.where(lq < HD, outs[0], outs[1]).astype(bf16)
        lse_ref[rows, :] = jnp.where(lq < HD, ls[0], ls[1])
        return 0
    lax.fori_loop(0, R//QB, body, 0)

def attn_fwd(proj, lengths, skew):
    _, L, W = proj.shape
    pairs = W // (PAIR)
    def sp(i): return pl.BlockSpec((None, L, PAIR), lambda p, i=i: (i, 0, p))
    return pl.pallas_call(fwd_kernel, grid=(pairs,),
        in_specs=[pl.BlockSpec(memory_space=pltpu.SMEM), sp(0), sp(1), sp(2),
                  pl.BlockSpec((2, QB, skew.shape[2]), lambda p:(p,0,0))],
        out_specs=[pl.BlockSpec((L, PAIR), lambda p:(0,p)), pl.BlockSpec((L, PAIR), lambda p:(0,p))],
        out_shape=[jax.ShapeDtypeStruct((L,W), bf16), jax.ShapeDtypeStruct((L,W), f32)],
        scratch_shapes=[pltpu.VMEM((2,L,PAIR), bf16), pltpu.VMEM((2,L,PAIR), bf16)],
        compiler_params=pltpu.CompilerParams(vmem_limit_bytes=VMEM_LIMIT), name="attn_fwd",
    )(lengths, proj, proj, proj, skew)

def bwd_kernel(len_ref, q_ref, k_ref, v_ref, do_ref, o_ref, lse_ref, t_ref,
               dq_ref, dk_ref, dv_ref, diag_ref, qx_ref, gx_ref, acc_ref, dqa_ref):
    L = k_ref.shape[0]
    W2 = PAIR
    lane = lax.broadcasted_iota(jnp.int32, (L, W2), 1)
    q = q_ref[...].astype(f32) * 0.125
    do = do_ref[...].astype(f32)
    prod = do * o_ref[...].astype(f32)
    lse = lse_ref[...]
    for h in range(2):
        own = (lane >= HD) if h else (lane < HD)
        first = 0 if h else HD
        delta = jnp.sum(jnp.where(own, prod, 0.0), axis=1, keepdims=True)
        l = lse[:, HD:HD+1] if h else lse[:, :1]
        la, lb, lc = split3(-l)
        qx_ref[h] = jnp.where(own, q, jnp.where(lane == first, 1.0, jnp.where(lane == first+1, la, jnp.where(lane == first+2, lb, jnp.where(lane == first+3, lc, 0.0))))).astype(bf16)
        da, db, dc = split3(-delta)
        gx_ref[h] = jnp.where(own, do, jnp.where(lane == first+1, da, jnp.where(lane == first+2, db, jnp.where(lane == first+3, dc, 0.0)))).astype(bf16)
    acc_ref[...] = jnp.zeros_like(acc_ref)
    lk = lax.broadcasted_iota(jnp.int32, (QB, W2), 1)
    rk = lax.broadcasted_iota(jnp.int32, (QB, W2), 0)
    def body(c, _):
        rows = pl.ds(pl.multiple_of(c*QB, QB), QB)
        k = k_ref[rows, :].astype(f32); v = v_ref[rows, :].astype(f32)
        mask = jnp.where(rk + c*QB < len_ref[0], 0.0, -1e9)
        start = pl.multiple_of(L - QB - c*QB, QB)
        dks=[]; dvs=[]; dqs=[]
        for h in range(2):
            own = (lk >= HD) if h else (lk < HD)
            first = 0 if h else HD
            kx = key_side(k, mask, own, lk, first)
            vx = jnp.where(own, v, jnp.where((lk > first) & (lk < first+4), 1.0, 0.0)).astype(bf16)
            s = lax.dot_general(kx, qx_ref[h], ROWS_BY_ROWS, preferred_element_type=f32)
            p = jnp.exp(s + t_ref[h, :, pl.ds(start, L)])
            dp = lax.dot_general(vx, gx_ref[h], ROWS_BY_ROWS, preferred_element_type=f32)
            ds = p * dp
            acc_ref[h, :, pl.ds(start, L)] += ds
            pb = p.astype(bf16); dsb = ds.astype(bf16)
            dvs.append(jnp.dot(pb, gx_ref[h], preferred_element_type=f32))
            dks.append(jnp.dot(dsb, qx_ref[h], preferred_element_type=f32))
            dqs.append(lax.dot_general(dsb, kx, COLS_BY_COLS, preferred_element_type=f32))
        dk_ref[rows, :] = jnp.where(lk < HD, dks[0], dks[1]).astype(bf16)
        dv_ref[rows, :] = jnp.where(lk < HD, dvs[0], dvs[1]).astype(bf16)
        dq = jnp.where(lane < HD, dqs[0], dqs[1])
        @pl.when(c == 0)
        def _(): dqa_ref[...] = dq
        @pl.when(c > 0)
        def _(): dqa_ref[...] += dq
        return 0
    lax.fori_loop(0, L//QB, body, 0)
    dq_ref[...] = (dqa_ref[...] * 0.125).astype(bf16)
    for h in range(2):
        diag_ref[h] = diagonal_sums(jnp.concatenate([acc_ref[h], jnp.zeros((QB, QB), f32)], axis=1))

def diagonal_sums(a):
    width = a.shape[1]
    total = pltpu.roll(a[:8], QB - 1, 1)
    for g in range(1, QB // 8):
        total = total + pltpu.roll(a[8*g : 8*g + 8], QB - 1 - 8*g, 1)
    sub = lax.broadcasted_iota(jnp.int32, total.shape, 0)
    for bit in (1, 2, 4):
        total = jnp.where((sub & bit) != 0, pltpu.roll(total, width - bit, 1), total)
    return jnp.sum(total, axis=0, keepdims=True)

def attn_bwd(proj, do, o, lse, lengths, skew_t):
    _, L, W = proj.shape
    pairs = W // (PAIR)
    def sp(i): return pl.BlockSpec((None, L, PAIR), lambda p, i=i: (i, 0, p))
    cs = pl.BlockSpec((L, PAIR), lambda p:(0,p))
    wid = skew_t.shape[2]
    return pl.pallas_call(bwd_kernel, grid=(pairs,),
        in_specs=[pl.BlockSpec(memory_space=pltpu.SMEM), sp(0), sp(1), sp(2), cs, cs, cs,
                  pl.BlockSpec((2, QB, wid), lambda p:(p,0,0))],
        out_specs=[cs, cs, cs, pl.BlockSpec((2, 1, wid+QB), lambda p:(p,0,0))],
        out_shape=[jax.ShapeDtypeStruct((L,W), bf16)]*3 + [jax.ShapeDtypeStruct((W//HD, 1, wid+QB), f32)],
        scratch_shapes=[pltpu.VMEM((2,L,PAIR), bf16), pltpu.VMEM((2,L,PAIR), bf16), pltpu.VMEM((2,QB,wid), f32), pltpu.VMEM((L,PAIR), f32)],
        compiler_params=pltpu.CompilerParams(vmem_limit_bytes=VMEM_LIMIT), name="attn_bwd",
    )(lengths, proj, proj, proj, do, o, lse, skew_t)

def unit(values):
    row_mean = jnp.mean(values, axis=-1, keepdims=True)
    centered = values - row_mean
    spread = jnp.mean(centered * centered, axis=-1, keepdims=True)
    inverse = lax.rsqrt(spread + 1e-05)
    return (centered * inverse, inverse)


def norm_back(grad_normed, unit_rows, inverse, gain_row):
    grad_unit = grad_normed * gain_row
    first_mean = jnp.mean(grad_unit, axis=-1, keepdims=True)
    second_mean = jnp.mean(grad_unit * unit_rows, axis=-1, keepdims=True)
    return inverse * (grad_unit - first_mean - unit_rows * second_mean)


def apply_update(weight, momentum, average, gradient, step_rate):
    next_moment = momentum_keep * momentum + gradient
    next_weight = weight - step_rate * (gradient + momentum_keep * next_moment)
    next_average = average_keep * average + (1.0 - average_keep) * next_weight
    return (next_moment, next_weight, next_average)


def swap(values, axis, bit):
    size = lax.axis_size(axis)
    return lax.ppermute(values, axis, [(i, i ^ bit) for i in range(size)])


def gather_rows(rows):
    if lax.axis_size("mp") != 2:
        return lax.all_gather(rows, "mp", axis=0, tiled=True)
    other = swap(rows, "mp", 1)
    first = lax.axis_index("mp") == 0
    return jnp.concatenate([jnp.where(first, rows, other), jnp.where(first, other, rows)], axis=0)


def sum_rows(rows):
    if lax.axis_size("mp") != 2:
        return lax.psum(rows, "mp").astype(f32)
    return rows.astype(f32) + swap(rows, "mp", 1).astype(f32)


def scatter_rows(rows):
    if lax.axis_size("mp") != 2:
        return lax.psum_scatter(rows, "mp", scatter_dimension=0, tiled=True).astype(f32)
    half = rows.shape[0] // 2
    mine = lax.axis_index("mp") * half
    sent = lax.dynamic_slice_in_dim(rows, half - mine, half, 0)
    kept = lax.dynamic_slice_in_dim(rows, mine, half, 0)
    return kept.astype(f32) + swap(sent, "mp", 1).astype(f32)


def halves_first(columns):
    rows, width = columns.shape
    bits = lax.axis_size("dp").bit_length() - 1
    split = columns.reshape((rows,) + (2,) * bits + (width >> bits,))
    order = (0,) + tuple(range(bits, 0, -1)) + (bits + 1,)
    return split.transpose(order).reshape(rows, 2, width >> 1)


def weight_share(ordered, right):
    place = lax.axis_index("dp")
    bits = lax.axis_size("dp").bit_length() - 1
    low = place & 1

    def product(which):
        piece = lax.dynamic_index_in_dim(ordered, which, 1, keepdims=False)
        return lax.dot_general(piece, right, COLS_BY_COLS, preferred_element_type=f32)

    got = swap(product(1 - low).astype(bf16), "dp", 1)
    total = product(low) + got.astype(f32)
    for bit in range(1, bits):
        total = total.astype(bf16)
        half = total.shape[0] // 2
        mine = (lax.shift_right_logical(place, bit) & 1) * half
        got = swap(lax.dynamic_slice_in_dim(total, half - mine, half, 0), "dp", 1 << bit)
        total = lax.dynamic_slice_in_dim(total, mine, half, 0).astype(f32) + got.astype(f32)
    return total


def sum_all(values):
    for axis in ("dp", "mp"):
        bit = 1
        while bit < lax.axis_size(axis):
            values = values + swap(values, axis, bit)
            bit *= 2
    return values


def gelu_parts(values):
    half_erf = 0.5 * lax.erf(values * 0.7071067811865476)
    gate = 0.5 + half_erf
    slope = gate + values * (0.3989422804014327 * jnp.exp(-0.5 * values * values))
    return (values * gate, slope)


def per_device(
    inputs,
    cotangent,
    lengths,
    buckets,
    w_qkv,
    w_out,
    w_ffn,
    norm_params,
    rel_bias,
    momentum_qkv,
    momentum_out,
    momentum_ffn,
    momentum_norms,
    momentum_bias,
    average_qkv,
    average_out,
    average_ffn,
    average_norms,
    average_bias,
):
    model_size = lax.axis_size("mp")
    data_size = lax.axis_size("dp")
    rows_local = inputs.shape[0]
    seq_len = rows_local * model_size
    width_local = w_qkv.shape[2]
    heads_local = width_local // HD
    head_first = lax.axis_index("mp") * heads_local
    own_first = lax.axis_index("mp") * rows_local
    data_index = lax.axis_index("dp")
    share_rows = momentum_out.shape[0]

    inputs_all = gather_rows(inputs).astype(f32)
    cot_all = gather_rows(cotangent)
    weights_qkv = w_qkv.astype(bf16)
    weights_out = w_out.astype(bf16)
    weights_ffn = w_ffn.astype(bf16)

    bias_local = lax.dynamic_slice_in_dim(rel_bias, head_first, heads_local, 1)
    bucket_hits = (buckets[:, None] == jnp.arange(rel_bias.shape[0], dtype=jnp.int32)[None, :]).astype(f32)
    bias_table = jnp.dot(bucket_hits, bias_local, precision=highest).T
    skew, skew_back = skew_tables(bias_table)

    unit_one, inverse_one = unit(inputs_all)
    normed_one = (unit_one * norm_params[0] + norm_params[1]).astype(bf16)
    projected = jnp.einsum("sd,tdc->tsc", normed_one, weights_qkv, preferred_element_type=f32).astype(bf16)
    context, log_totals = attn_fwd(projected, lengths, skew)
    branch = lax.dot_general(context, weights_out, ROWS_BY_ROWS, preferred_element_type=f32).astype(bf16)
    middle = inputs_all + sum_rows(branch)
    unit_two, inverse_two = unit(middle)
    normed_two = (unit_two * norm_params[2] + norm_params[3]).astype(bf16)

    hidden_pre = jnp.dot(normed_two, weights_ffn[0], preferred_element_type=f32)
    hidden, slope = gelu_parts(hidden_pre)
    hidden = hidden.astype(bf16)
    hidden_grad = jnp.dot(cot_all, weights_ffn[1], preferred_element_type=f32)
    pre_grad = (hidden_grad * slope).astype(bf16)
    normed_two_part = lax.dot_general(pre_grad, weights_ffn[0], ROWS_BY_ROWS, preferred_element_type=f32).astype(bf16)
    normed_two_grad = sum_rows(normed_two_part)
    out_part = lax.dot_general(hidden, weights_ffn[1], ROWS_BY_ROWS, preferred_element_type=f32).astype(bf16)
    middle_own = lax.dynamic_slice_in_dim(middle, own_first, rows_local, 0)
    output = (middle_own + scatter_rows(out_part)).astype(bf16)

    up_share = weight_share(halves_first(normed_two), pre_grad)
    down_share = weight_share(halves_first(cot_all), hidden)

    middle_grad = cot_all.astype(f32) + norm_back(normed_two_grad, unit_two, inverse_two, norm_params[2])
    gain_two_grad = jnp.sum(normed_two_grad * unit_two, axis=0) / model_size
    shift_two_grad = jnp.sum(normed_two_grad, axis=0) / model_size
    branch_grad = middle_grad.astype(bf16)
    context_grad = jnp.dot(branch_grad, weights_out, preferred_element_type=f32).astype(bf16)
    out_share = weight_share(halves_first(branch_grad), context)

    query_grad, key_grad, value_grad, diagonals = attn_bwd(projected, context_grad, context, log_totals, lengths, skew_back)
    offset_grad = diagonals[:, 0, : 2 * seq_len - 1]
    ordered_one = halves_first(normed_one)
    grad_parts = [query_grad, key_grad, value_grad]
    normed_one_part = sum(
        lax.dot_general(g, weights_qkv[t], ROWS_BY_ROWS, preferred_element_type=f32) for t, g in enumerate(grad_parts)
    )
    gain_one_grad = jnp.sum(normed_one_part * unit_one, axis=0)
    shift_one_grad = jnp.sum(normed_one_part, axis=0)
    normed_one_grad = scatter_rows(normed_one_part.astype(bf16))
    qkv_share = weight_share(ordered_one, jnp.concatenate(grad_parts, axis=1))
    qkv_share = qkv_share.reshape(share_rows, 3, width_local).transpose(1, 0, 2)

    unit_own, inverse_own = unit(inputs.astype(f32))
    input_grad = lax.dynamic_slice_in_dim(middle_grad, own_first, rows_local, 0) + norm_back(
        normed_one_grad, unit_own, inverse_own, norm_params[0]
    )

    bias_grad_local = jnp.einsum("rb,hr->bh", bucket_hits[::-1], offset_grad, precision=highest)
    bias_grad_full = lax.dynamic_update_slice_in_dim(jnp.zeros(rel_bias.shape, f32), bias_grad_local, head_first, 1)
    norm_grad_local = jnp.stack([gain_one_grad, shift_one_grad, gain_two_grad, shift_two_grad])
    small = jnp.concatenate([norm_grad_local.reshape(-1, 128), bias_grad_full.reshape(-1, 128)], axis=0)
    small = sum_all(small)
    norm_rows = norm_grad_local.size // 128
    norm_grad = small[:norm_rows].reshape(norm_grad_local.shape)
    bias_grad = small[norm_rows:].reshape(rel_bias.shape)

    ffn_share = jnp.stack([up_share, down_share])
    scale_factor = 1.0 / math.sqrt(float(seq_len * data_size))
    weight_qkv_share = lax.dynamic_slice_in_dim(w_qkv, data_index * share_rows, share_rows, 1)
    weight_out_share = lax.dynamic_slice_in_dim(w_out, data_index * share_rows, share_rows, 0)
    weight_ffn_share = lax.dynamic_slice_in_dim(w_ffn, data_index * share_rows, share_rows, 1)
    moment_qkv, weight_qkv, mean_qkv = apply_update(
        weight_qkv_share, momentum_qkv, average_qkv, qkv_share, 0.3 * scale_factor
    )
    moment_out, weight_out, mean_out = apply_update(
        weight_out_share, momentum_out, average_out, out_share, 0.1 * scale_factor
    )
    moment_ffn, weight_ffn, mean_ffn = apply_update(
        weight_ffn_share, momentum_ffn, average_ffn, ffn_share, 0.05 * scale_factor
    )
    moment_norms, weight_norms, mean_norms = apply_update(
        norm_params, momentum_norms, average_norms, norm_grad, 0.05 * scale_factor
    )
    moment_bias, weight_bias, mean_bias = apply_update(
        rel_bias, momentum_bias, average_bias, bias_grad, 0.05 * scale_factor
    )
    return (
        output,
        input_grad,
        qkv_share,
        moment_qkv,
        weight_qkv,
        mean_qkv,
        out_share,
        moment_out,
        weight_out,
        mean_out,
        ffn_share,
        moment_ffn,
        weight_ffn,
        mean_ffn,
        norm_grad,
        moment_norms,
        weight_norms,
        mean_norms,
        bias_grad,
        moment_bias,
        weight_bias,
        mean_bias,
    )


def solution(mesh):
    return jax.shard_map(
        per_device,
        mesh=mesh,
        in_specs=(
            P(("dp", "mp"), None),
            P(("dp", "mp"), None),
            P("dp"),
            P(),
            P(None, None, "mp"),
            P(None, "mp"),
            P(None, None, "mp"),
            P(),
            P(),
            P(None, "dp", "mp"),
            P("dp", "mp"),
            P(None, "dp", "mp"),
            P(),
            P(),
            P(None, "dp", "mp"),
            P("dp", "mp"),
            P(None, "dp", "mp"),
            P(),
            P(),
        ),
        out_specs=(
            P(("dp", "mp"), None),
            P(("dp", "mp"), None),
            P(None, "dp", "mp"),
            P(None, "dp", "mp"),
            P(None, "dp", "mp"),
            P(None, "dp", "mp"),
            P("dp", "mp"),
            P("dp", "mp"),
            P("dp", "mp"),
            P("dp", "mp"),
            P(None, "dp", "mp"),
            P(None, "dp", "mp"),
            P(None, "dp", "mp"),
            P(None, "dp", "mp"),
            P(),
            P(),
            P(),
            P(),
            P(),
            P(),
            P(),
            P(),
        ),
        check_vma=False,
    )
```

time: 1650 us -> 463 us (0.28)
  local copies, waits for them, and re-layouts: 800 us -> 49.5 us
  waiting for transfers between devices: 416 us -> 146 us
  matrix products: 209 us -> 78.7 us
  Pallas kernels: 0 us -> 87.3 us
  other arithmetic: 138 us -> 61.2 us
  blocking collectives: 41.4 us -> 0 us
  starting transfers between devices: 0.54 us -> 28.5 us
    while x65 -> x0, local copies, waits for them, and re-layouts: 323 us -> none
    reshape x8, local copies, waits for them, and re-layouts: 204 us -> 4.37 us  [the longest x3 2.02 us: halves_first(): split = columns.reshape((rows,) + (2,) * bits + (width >> bits,))]
    psum x1 -> x0, waiting for transfers between devices: 186 us -> none  [per_device(): lax.psum(qkv_weight_grad.astype(jnp.bfloat16), 'dp').astype(jnp.float32)]
    another operation x14 -> x0, local copies, waits for them, and re-layouts: 153 us -> none  [the longest x8 142 us: skew_bias(): tiled = jnp.tile(piece, (1, block_rows))]
    ppermute x0 -> x27, waiting for transfers between devices: none -> 146 us  [swap(): return lax.ppermute(values, axis, [(i, i ^ bit) for i in range(size)])]
    reduce_scatter x4 -> x0, waiting for transfers between devices: 131 us -> none  [the longest x1 54.4 us: per_device(): lax.psum_scatter(jnp.einsum('sc,dc->sd', row_piece, weights_out, preferre...]
    dot_general x27 -> x19, matrix products: 207 us -> 77.8 us  [the longest x8 27.8 us: product(): lax.dot_general(piece, right, COLS_BY_COLS, preferred_element_type=f32)]
    all_gather x4 -> x0, waiting for transfers between devices: 99.3 us -> none  [the longest x1 34.5 us: per_device(): lax.all_gather(normed_one.astype(jnp.bfloat16), 'mp', axis=0, tiled=True)]
  transfers between devices with their start and end apart: 9 -> 27, of which waited for: 8 -> 14; matrix products, arithmetic and copies ran while one was open for 6% -> 30% of each run, Pallas kernels for 0% -> 12%
where the time goes in v1:
time: 463 us; the launch traced here: 454 us
  waiting for transfers between devices  146 us (32%)
  Pallas kernels  87.3 us (19%)
  matrix products  78.7 us (17%)
  other arithmetic  61.2 us (13%)
  local copies, waits for them, and re-layouts  49.5 us (11%)
  starting transfers between devices  28.5 us (6%)
    ppermute x27, waiting for transfers between devices, swap(): return lax.ppermute(values, axis, [(i, i ^ bit) for i in range(size)])  146 us
    pallas_call x1, Pallas kernels, attn_bwd(): pl.pallas_call(bwd_kernel, grid=(pairs,), in_specs=[pl.BlockSpec(memory_s...  45.6 us
    pallas_call x1, Pallas kernels, attn_fwd(): pl.pallas_call(fwd_kernel, grid=(pairs,), in_specs=[pl.BlockSpec(memory_s...  33.3 us
    ppermute x27, starting transfers between devices, swap(): return lax.ppermute(values, axis, [(i, i ^ bit) for i in range(size)])  28.5 us
    dot_general x8, matrix products, product(): lax.dot_general(piece, right, COLS_BY_COLS, preferred_element_type=f32)  27.8 us
    unnamed x138, local copies, waits for them, and re-layouts  25.4 us
    add x5, other arithmetic, apply_update(): next_average = average_keep * average + (1.0 - average_keep) * next_weight  9.27 us
  transfers between devices with their start and end apart: 27, of which 14 were waited for; matrix products, arithmetic and copies ran while one was open for 30% of the time, Pallas kernels for 12%

profile of v1, /device:TPU:0, one launch (start us, length us, event | category | flops | bytes accessed | tf_op | source)
XLA Modules:
  0.0 454.4 jit_solution(4856689913188793357)
XLA Ops:
  7.8 4.9 %convert_element_type.226 = bf16[3,1024,512]{2,1,0:T(8,128)(2,1)} convert(f32[3,1024,512]{2,1,0:T(8,128)} %param.23) | non-fusion elementwise | flops 1572864 | bytes 9437184 | tf_op jit(solution)/shard_map/convert_element_type | solution.py:305
  16.2 8.4 %skew.1 = (f32[8,128,1920]{2,1,0:T(8,128)}, f32[8,128,1920]{2,1,0:T(8,128)}) custom-call(f32[8,1,2048]{2,1,0:T(1,128)} %broadcast_in_dim.6.tab_ref, f32[8,1,2048]{2,1,0:T(1,128)} %broadcast_in_dim.7.rev_ref), custom_call_target="tpu_custom_call" | custom-call | tf_op jit(solution)/shard_map/skew/pallas_call | solution.py:39
  25.2 4.0 collective-permute-done.3
  30.2 20.8 %collective-permute-done = bf16[512,1024]{0,1:T(8,128)(2,1)} collective-permute-done((bf16[512,1024]{0,1:T(8,128)(2,1)S(1)}, bf16[512,1024]{0,1:T(8,128)(2,1)}, u32[]{:S(2)}, u32[]{:S(2)}) %collective-permute-start) | collective-permute-done | bytes 1048608 | tf_op jit(solution)/shard_map/ppermute | solution.py:200
  56.3 5.4 %convert_bitcast_fusion.q_ref.k_ref.v_ref = bf16[3,1024,512]{2,1,0:T(8,128)(2,1)} fusion(bf16[3,1024,512]{2,1,0:T(8,128)(2,1)S(1)} %copy-done.7, f32[1024]{0:T(1024)S(1)} %bitcast.155, f32[1024]{0:T(1024)S(1)} %bitcast.149, f32[1024]{0:T(1024)S(1)} %add_rsqrt_fusion.1, f32[1024]{0:T(1024)S(1)} %broadcast_multiply_fusion.5, ...), kind=kOutput, calls=%fused_computation.40 | convolution fusion | flops 3232235520 | bytes 8404992 | tf_op jit(solution)/shard_map/sd,tdc->tsc/dot_general | solution.py:316
  61.7 33.3 %attn_fwd.1 = (bf16[1024,512]{1,0:T(8,128)(2,1)}, f32[1024,512]{1,0:T(8,128)}) custom-call(s32[1]{0:T(128)S(6)} %copy.130.len_ref, bf16[3,1024,512]{2,1,0:T(8,128)(2,1)} %convert_bitcast_fusion.q_ref.k_ref.v_ref, bf16[3,1024,512]{2,1,0:T(8,128)(2,1)} %convert_bitcast_fusion.q_ref.k_ref.v_ref, bf16[3,1024,512]{2,1,0:T(8,128)(2,1)} %convert_bitcast_fusion.q_ref.k_ref.v_ref, ...), custom_call_target="tpu_custom_call" | custom-call | tf_op jit(solution)/shard_map/attn_fwd/pallas_call | solution.py:88
  101.2 9.1 %convert_element_type.234 = bf16[2,1024,2048]{2,1,0:T(8,128)(2,1)} convert(f32[2,1024,2048]{2,1,0:T(8,128)} %param.25) | non-fusion elementwise | flops 4194304 | bytes 25165824 | tf_op jit(solution)/shard_map/convert_element_type | solution.py:307
  112.9 9.1 %rev.7 = f32[2047,32]{1,0:T(8,128)} reverse(f32[2047,32]{1,0:T(8,128)} %fusion.68), dimensions={0} | reverse | bytes 524032 | tf_op jit(solution)/shard_map/rev | solution.py:362
  130.2 15.8 %collective-permute-done.1 = bf16[1024,1024]{0,1:T(8,128)(2,1)} collective-permute-done((bf16[1024,1024]{0,1:T(8,128)(2,1)}, bf16[1024,1024]{0,1:T(8,128)(2,1)}, u32[]{:S(2)}, u32[]{:S(2)}) %collective-permute-start.1) | collective-permute-done | bytes 2097184 | tf_op jit(solution)/shard_map/ppermute | solution.py:200
  153.3 7.8 %multiply_convert_fusion = (bf16[1024,2048]{1,0:T(8,128)(2,1)}, f32[1024,2048]{1,0:T(8,128)}) fusion(bf16[1024,1024]{0,1:T(8,128)(2,1)S(1)} %add_convert_fusion.3, bf16[2,1024,2048]{2,1,0:T(8,128)(2,1)S(1)} %bitcast.131), kind=kOutput, calls=%fused_computation.7 | convolution fusion | flops 4305453056 | bytes 18874368 | tf_op jit(solution)/shard_map/dot_general | solution.py:323
  161.1 8.9 %fusion.5 = bf16[1024,2048]{1,0:T(8,128)(2,1)S(1)} fusion(f32[1024,2048]{1,0:T(8,128)} %get-tuple-element.123, bf16[2,1024,2048]{2,1,0:T(8,128)(2,1)S(1)} %bitcast.131, bf16[512,1024]{0,1:T(8,128)(2,1)S(1)} %copy-done.5, bf16[512,1024]{0,1:T(8,128)(2,1)S(1)} %copy-done.3), kind=kOutput, calls=%fused_computation.6 | convolution fusion | flops 4320133120 | bytes 18874368 | tf_op jit(solution)/shard_map/dot_general | solution.py:326
  170.0 5.8 %fusion.36 = bf16[1024,1024]{0,1:T(8,128)(2,1)} fusion(bf16[1024,2048]{1,0:T(8,128)(2,1)S(1)} %fusion.5, bf16[2,1024,2048]{2,1,0:T(8,128)(2,1)S(1)} %bitcast.131), kind=kOutput, calls=%fused_computation.68 | convolution fusion | flops 4296015872 | bytes 10485760 | tf_op jit(solution)/shard_map/dot_general | solution.py:328
  177.2 7.3 %fusion.35 = bf16[1024,1024]{0,1:T(8,128)(2,1)S(1)} fusion(bf16[1024,2048]{1,0:T(8,128)(2,1)} %get-tuple-element.122, bf16[2,1024,2048]{2,1,0:T(8,128)(2,1)S(1)} %bitcast.131), kind=kOutput, calls=%fused_computation.67 | convolution fusion | flops 4296015872 | bytes 10485760 | tf_op jit(solution)/shard_map/dot_general | solution.py:330
  185.3 5.9 %convolution_convert_fusion = bf16[512,2048]{1,0:T(8,128)(2,1)} fusion(bf16[1024,2048]{1,0:T(8,128)(2,1)} %get-tuple-element.122, bf16[1024,2,512]{0,2,1:T(8,128)(2,1)S(1)} %bitcast.140, s32[]{:T(128)S(6)} %select_n.97), kind=kOutput, calls=%fused_computation.41 | convolution fusion | flops 2148532224 | bytes 7340036 | tf_op jit(solution)/shard_map/dot_general | solution.py:242
  195.7 48.7 %collective-permute-done.2 = bf16[512,1024]{0,1:T(8,128)(2,1)S(1)} collective-permute-done((bf16[512,1024]{0,1:T(8,128)(2,1)S(1)}, bf16[512,1024]{0,1:T(8,128)(2,1)S(1)}, u32[]{:S(2)}, u32[]{:S(2)}) %collective-permute-start.2) | collective-permute-done | bytes 1048608 | tf_op jit(solution)/shard_map/ppermute | solution.py:200
  248.1 5.3 %multiply_reduce_fusion = (f32[1024]{0:T(1024)S(1)}, f32[1024]{0:T(1024)S(1)}, f32[1024]{0:T(1024)S(1)}, f32[1024]{0:T(1024)S(1)}) fusion(bf16[1024,1024]{0,1:T(8,128)(2,1)} %collective-permute-done.4, bf16[1024,1024]{0,1:T(8,128)(2,1)} %fusion.36, f32[1024,1024]{0,1:T(8,128)} %copy-done, f32[1024]{0:T(1024)S(1)} %add_rsqrt_fusion, ...), kind=kLoop, calls=%fused_computation.22 | loop fusion | flops 12578816 | bytes 8417280 | tf_op jit(solution)/shard_map/reduce_sum | solution.py:338
  253.5 5.2 %fusion.86 = (bf16[1024,1024]{0,1:T(8,128)(2,1)S(1)}, f32[1024,1024]{0,1:T(8,128)}) fusion(f32[1024]{0:T(1024)S(1)} %broadcast_multiply_fusion.2, f32[1024,1024]{0,1:T(8,128)S(1)} %copy-done.1, f32[1024]{0:T(1024)S(1)} %broadcast_multiply_fusion.4, f32[1024]{0:T(1024)S(1)} %broadcast_multiply_fusion.3, f32[1024]{0:T(1024)S(1)} %bitcast.148, ...), kind=kLoop, calls=%fused_computation.184 | loop fusion | flops 16777216 | bytes 16797696 | tf_op jit(solution)/shard_map/convert_element_type | solution.py:340
  260.9 45.6 %attn_bwd.1 = (bf16[1024,512]{1,0:T(8,128)(2,1)}, bf16[1024,512]{1,0:T(8,128)(2,1)}, bf16[1024,512]{1,0:T(8,128)(2,1)}, f32[8,1,2048]{2,1,0:T(1,128)}) custom-call(s32[1]{0:T(128)S(6)} %copy.130.len_ref, bf16[3,1024,512]{2,1,0:T(8,128)(2,1)} %convert_bitcast_fusion.q_ref.k_ref.v_ref, bf16[3,1024,512]{2,1,0:T(8,128)(2,1)} %convert_bitcast_fusion.q_ref.k_ref.v_ref, ...), custom_call_target="tpu_custom_call" | custom-call | tf_op jit(solution)/shard_map/attn_bwd/pallas_call | solution.py:167
  328.5 5.5 %add_convert_fusion = bf16[512,2048]{1,0:T(8,128)(2,1)S(1)} fusion(bf16[512,2048]{1,0:T(8,128)(2,1)} %collective-permute-done.18, bf16[1024,2048]{1,0:T(8,128)(2,1)} %get-tuple-element.122, bf16[1024,2,512]{0,2,1:T(8,128)(2,1)} %bitcast.141, s32[]{:T(128)S(6)} %select_n.96), kind=kOutput, calls=%fused_computation.23 | convolution fusion | flops 2150629376 | bytes 9437188 | tf_op jit(solution)/shard_map/dot_general | solution.py:242
  344.2 4.0 add_convert_fusion.1
  354.6 15.4 %collective-permute-done.11 = bf16[256,512]{1,0:T(8,128)(2,1)} collective-permute-done((bf16[256,512]{1,0:T(8,128)(2,1)}, bf16[256,512]{1,0:T(8,128)(2,1)}, u32[]{:S(2)}, u32[]{:S(2)}) %collective-permute-start.11) | collective-permute-done | bytes 262176 | tf_op jit(solution)/shard_map/ppermute | solution.py:200
  405.2 9.3 %collective-permute-done.20 = bf16[128,2048]{1,0:T(8,128)(2,1)S(1)} collective-permute-done((bf16[128,2048]{1,0:T(8,128)(2,1)S(1)}, bf16[128,2048]{1,0:T(8,128)(2,1)S(1)}, u32[]{:S(2)}, u32[]{:S(2)}) %collective-permute-start.20) | collective-permute-done | bytes 524320 | tf_op jit(solution)/shard_map/ppermute | solution.py:200
  414.8 12.0 %collective-permute-done.16 = bf16[128,2048]{1,0:T(8,128)(2,1)S(1)} collective-permute-done((bf16[128,2048]{1,0:T(8,128)(2,1)S(1)}, bf16[128,2048]{1,0:T(8,128)(2,1)S(1)}, u32[]{:S(2)}, u32[]{:S(2)}) %collective-permute-start.16) | collective-permute-done | bytes 524320 | tf_op jit(solution)/shard_map/ppermute | solution.py:200
  429.6 9.2 %collective-permute-done.17 = bf16[64,2048]{1,0:T(8,128)(2,1)S(1)} collective-permute-done((bf16[64,2048]{1,0:T(8,128)(2,1)S(1)}, bf16[64,2048]{1,0:T(8,128)(2,1)S(1)}, u32[]{:S(2)}, u32[]{:S(2)}) %collective-permute-start.17) | collective-permute-done | bytes 262176 | tf_op jit(solution)/shard_map/ppermute | solution.py:200
  (283 shorter events, 145.2 us)
Async XLA Ops:
  2.2 27.0 %collective-permute-start.3 = (bf16[512,1024]{0,1:T(8,128)(2,1)S(1)}, bf16[512,1024]{0,1:T(8,128)(2,1)S(1)}, u32[]{:S(2)}, u32[]{:S(2)}) collective-permute-start(bf16[512,1024]{0,1:T(8,128)(2,1)S(1)} %copy.62), channel_id=1, source_target_pairs={{0,1},{1,0},{2,3},{3,2},{4,5},{5,4},{6,7},{7,6},{8,9},{9,8},{10,11... | collective-permute-start | bytes 3145736 | tf_op jit(solution)/shard_map/ppermute | solution.py:200
  6.7 44.2 %collective-permute-start = (bf16[512,1024]{0,1:T(8,128)(2,1)S(1)}, bf16[512,1024]{0,1:T(8,128)(2,1)}, u32[]{:S(2)}, u32[]{:S(2)}) collective-permute-start(bf16[512,1024]{0,1:T(8,128)(2,1)S(1)} %copy.57), channel_id=1, source_target_pairs={{0,1},{1,0},{2,3},{3,2},{4,5},{5,4},{6,7},{7,6},{8,9},{9,8},{10,11... | collective-permute-start | bytes 3145736 | tf_op jit(solution)/shard_map/ppermute | solution.py:200
  98.8 47.1 %collective-permute-start.1 = (bf16[1024,1024]{0,1:T(8,128)(2,1)}, bf16[1024,1024]{0,1:T(8,128)(2,1)}, u32[]{:S(2)}, u32[]{:S(2)}) collective-permute-start(bf16[1024,1024]{0,1:T(8,128)(2,1)} %convolution_convert_fusion.3), channel_id=1, source_target_pairs={{0,1},{1,0},{2,3},{3,2},{4,5},{5,4},{6,7},{7,6},{8,9},{9,8},{10,11... | collective-permute-start | bytes 6291464 | tf_op jit(solution)/shard_map/ppermute | solution.py:200
  175.8 72.3 %collective-permute-start.4 = (bf16[1024,1024]{0,1:T(8,128)(2,1)}, bf16[1024,1024]{0,1:T(8,128)(2,1)}, u32[]{:S(2)}, u32[]{:S(2)}) collective-permute-start(bf16[1024,1024]{0,1:T(8,128)(2,1)} %fusion.36), channel_id=1, source_target_pairs={{0,1},{1,0},{2,3},{3,2},{4,5},{5,4},{6,7},{7,6},{8,9},{9,8},{10,11... | collective-permute-start | bytes 6291464 | tf_op jit(solution)/shard_map/ppermute | solution.py:200
  184.6 59.7 %collective-permute-start.2 = (bf16[512,1024]{0,1:T(8,128)(2,1)S(1)}, bf16[512,1024]{0,1:T(8,128)(2,1)S(1)}, u32[]{:S(2)}, u32[]{:S(2)}) collective-permute-start(bf16[512,1024]{0,1:T(8,128)(2,1)S(1)} %constant_dynamic-slice_fusion.14), channel_id=1, source_target_pairs={{0,1},{1,0},{2,3},{3,2},{4,5},{5,4},{6,7},{7,6},{8,9},{9,8},{10,11... | collective-permute-start | bytes 3145736 | tf_op jit(solution)/shard_map/ppermute | solution.py:200
  191.2 136.0 %collective-permute-start.18 = (bf16[512,2048]{1,0:T(8,128)(2,1)}, bf16[512,2048]{1,0:T(8,128)(2,1)}, u32[]{:S(2)}, u32[]{:S(2)}) collective-permute-start(bf16[512,2048]{1,0:T(8,128)(2,1)} %convolution_convert_fusion), channel_id=1, source_target_pairs={{0,2},{2,0},{4,6},{6,4},{8,10},{10,8},{12,14},{14,12},{16,18},{18,... | collective-permute-start | bytes 6291464 | tf_op jit(solution)/shard_map/ppermute | solution.py:200
  195.2 147.5 %collective-permute-start.14 = (bf16[512,2048]{1,0:T(8,128)(2,1)}, bf16[512,2048]{1,0:T(8,128)(2,1)}, u32[]{:S(2)}, u32[]{:S(2)}) collective-permute-start(bf16[512,2048]{1,0:T(8,128)(2,1)} %convolution_convert_fusion.1), channel_id=1, source_target_pairs={{0,2},{2,0},{4,6},{6,4},{8,10},{10,8},{12,14},{14,12},{16,18},{18,... | collective-permute-start | bytes 6291464 | tf_op jit(solution)/shard_map/ppermute | solution.py:200
  313.9 75.0 %collective-permute-start.5 = (bf16[512,1024]{0,1:T(8,128)(2,1)}, bf16[512,1024]{0,1:T(8,128)(2,1)}, u32[]{:S(2)}, u32[]{:S(2)}) collective-permute-start(bf16[512,1024]{0,1:T(8,128)(2,1)} %constant_dynamic-slice_fusion.13), channel_id=1, source_target_pairs={{0,1},{1,0},{2,3},{3,2},{4,5},{5,4},{6,7},{7,6},{8,9},{9,8},{10,11... | collective-permute-start | bytes 3145736 | tf_op jit(solution)/shard_map/ppermute | solution.py:200
  318.5 83.0 %collective-permute-start.6 = (bf16[512,1536]{1,0:T(8,128)(2,1)}, bf16[512,1536]{1,0:T(8,128)(2,1)}, u32[]{:S(2)}, u32[]{:S(2)}) collective-permute-start(bf16[512,1536]{1,0:T(8,128)(2,1)} %convolution_convert_fusion.2), channel_id=1, source_target_pairs={{0,2},{2,0},{4,6},{6,4},{8,10},{10,8},{12,14},{14,12},{16,18},{18,... | collective-permute-start | bytes 4718600 | tf_op jit(solution)/shard_map/ppermute | solution.py:200
  327.1 11.6 %collective-permute-start.10 = (bf16[512,512]{1,0:T(8,128)(2,1)S(1)}, bf16[512,512]{1,0:T(8,128)(2,1)S(1)}, u32[]{:S(2)}, u32[]{:S(2)}) collective-permute-start(bf16[512,512]{1,0:T(8,128)(2,1)S(1)} %convolution_convert_fusion.5), channel_id=1, source_target_pairs={{0,2},{2,0},{4,6},{6,4},{8,10},{10,8},{12,14},{14,12},{16,18},{18,... | collective-permute-start | bytes 1572872 | tf_op jit(solution)/shard_map/ppermute | solution.py:200
  327.2 6.9 %collective-permute-start.23 = (f32[36,128]{1,0:T(8,128)S(1)}, f32[36,128]{1,0:T(8,128)S(1)}, u32[]{:S(2)}, u32[]{:S(2)}) collective-permute-start(f32[36,128]{1,0:T(8,128)S(1)} %add.342), channel_id=1, source_target_pairs={{0,4},{2,6},{4,0},{6,2},{8,12},{10,14},{12,8},{14,10},{16,20},{18,... | collective-permute-start | bytes 55304 | tf_op jit(solution)/shard_map/ppermute | solution.py:200
  338.0 57.5 %collective-permute-start.19 = (bf16[256,2048]{1,0:T(8,128)(2,1)}, bf16[256,2048]{1,0:T(8,128)(2,1)}, u32[]{:S(2)}, u32[]{:S(2)}) collective-permute-start(bf16[256,2048]{1,0:T(8,128)(2,1)} %constant_dynamic-slice_fusion.2), channel_id=1, source_target_pairs={{0,4},{2,6},{4,0},{6,2},{8,12},{10,14},{12,8},{14,10},{16,20},{18,... | collective-permute-start | bytes 3145736 | tf_op jit(solution)/shard_map/ppermute | solution.py:200
  338.7 9.5 %collective-permute-start.25 = (f32[36,128]{1,0:T(8,128)S(1)}, f32[36,128]{1,0:T(8,128)S(1)}, u32[]{:S(2)}, u32[]{:S(2)}) collective-permute-start(f32[36,128]{1,0:T(8,128)S(1)} %add.344), channel_id=1, source_target_pairs={{0,16},{2,18},{4,20},{6,22},{8,24},{10,26},{12,28},{14,30},{16,0},... | collective-permute-start | bytes 55304 | tf_op jit(solution)/shard_map/ppermute | solution.py:200
  342.7 27.3 %collective-permute-start.11 = (bf16[256,512]{1,0:T(8,128)(2,1)}, bf16[256,512]{1,0:T(8,128)(2,1)}, u32[]{:S(2)}, u32[]{:S(2)}) collective-permute-start(bf16[256,512]{1,0:T(8,128)(2,1)} %constant_dynamic-slice_fusion.8), channel_id=1, source_target_pairs={{0,4},{2,6},{4,0},{6,2},{8,12},{10,14},{12,8},{14,10},{16,20},{18,... | collective-permute-start | bytes 786440 | tf_op jit(solution)/shard_map/ppermute | solution.py:200
  352.1 46.6 %collective-permute-start.15 = (bf16[256,2048]{1,0:T(8,128)(2,1)}, bf16[256,2048]{1,0:T(8,128)(2,1)}, u32[]{:S(2)}, u32[]{:S(2)}) collective-permute-start(bf16[256,2048]{1,0:T(8,128)(2,1)} %constant_dynamic-slice_fusion.5), channel_id=1, source_target_pairs={{0,4},{2,6},{4,0},{6,2},{8,12},{10,14},{12,8},{14,10},{16,20},{18,... | collective-permute-start | bytes 3145736 | tf_op jit(solution)/shard_map/ppermute | solution.py:200
  371.1 5.0 %collective-permute-start.12 = (bf16[128,512]{1,0:T(8,128)(2,1)S(1)}, bf16[128,512]{1,0:T(8,128)(2,1)S(1)}, u32[]{:S(2)}, u32[]{:S(2)}) collective-permute-start(bf16[128,512]{1,0:T(8,128)(2,1)S(1)} %constant_dynamic-slice_fusion.7), channel_id=1, source_target_pairs={{0,8},{2,10},{4,12},{6,14},{8,0},{10,2},{12,4},{14,6},{16,24},{18,... | collective-permute-start | bytes 393224 | tf_op jit(solution)/shard_map/ppermute | solution.py:200
  377.5 9.4 %collective-permute-start.13 = (bf16[64,512]{1,0:T(8,128)(2,1)}, bf16[64,512]{1,0:T(8,128)(2,1)}, u32[]{:S(2)}, u32[]{:S(2)}) collective-permute-start(bf16[64,512]{1,0:T(8,128)(2,1)} %constant_dynamic-slice_fusion.6), channel_id=1, source_target_pairs={{0,16},{2,18},{4,20},{6,22},{8,24},{10,26},{12,28},{14,30},{16,0},... | collective-permute-start | bytes 196616 | tf_op jit(solution)/shard_map/ppermute | solution.py:200
  397.6 16.9 %collective-permute-start.20 = (bf16[128,2048]{1,0:T(8,128)(2,1)S(1)}, bf16[128,2048]{1,0:T(8,128)(2,1)S(1)}, u32[]{:S(2)}, u32[]{:S(2)}) collective-permute-start(bf16[128,2048]{1,0:T(8,128)(2,1)S(1)} %constant_dynamic-slice_fusion.1), channel_id=1, source_target_pairs={{0,8},{2,10},{4,12},{6,14},{8,0},{10,2},{12,4},{14,6},{16,24},{18,... | collective-permute-start | bytes 1572872 | tf_op jit(solution)/shard_map/ppermute | solution.py:200
  400.4 26.4 %collective-permute-start.16 = (bf16[128,2048]{1,0:T(8,128)(2,1)S(1)}, bf16[128,2048]{1,0:T(8,128)(2,1)S(1)}, u32[]{:S(2)}, u32[]{:S(2)}) collective-permute-start(bf16[128,2048]{1,0:T(8,128)(2,1)S(1)} %constant_dynamic-slice_fusion.4), channel_id=1, source_target_pairs={{0,8},{2,10},{4,12},{6,14},{8,0},{10,2},{12,4},{14,6},{16,24},{18,... | collective-permute-start | bytes 1572872 | tf_op jit(solution)/shard_map/ppermute | solution.py:200
  404.7 23.4 %collective-permute-start.7 = (bf16[256,1536]{1,0:T(8,128)(2,1)S(1)}, bf16[256,1536]{1,0:T(8,128)(2,1)S(1)}, u32[]{:S(2)}, u32[]{:S(2)}) collective-permute-start(bf16[256,1536]{1,0:T(8,128)(2,1)S(1)} %constant_dynamic-slice_fusion.12), channel_id=1, source_target_pairs={{0,4},{2,6},{4,0},{6,2},{8,12},{10,14},{12,8},{14,10},{16,20},{18,... | collective-permute-start | bytes 2359304 | tf_op jit(solution)/shard_map/ppermute | solution.py:200
  414.7 13.5 %collective-permute-start.21 = (bf16[64,2048]{1,0:T(8,128)(2,1)S(1)}, bf16[64,2048]{1,0:T(8,128)(2,1)S(1)}, u32[]{:S(2)}, u32[]{:S(2)}) collective-permute-start(bf16[64,2048]{1,0:T(8,128)(2,1)S(1)} %constant_dynamic-slice_fusion), channel_id=1, source_target_pairs={{0,16},{2,18},{4,20},{6,22},{8,24},{10,26},{12,28},{14,30},{16,0},... | collective-permute-start | bytes 786440 | tf_op jit(solution)/shard_map/ppermute | solution.py:200
  426.9 11.9 %collective-permute-start.17 = (bf16[64,2048]{1,0:T(8,128)(2,1)S(1)}, bf16[64,2048]{1,0:T(8,128)(2,1)S(1)}, u32[]{:S(2)}, u32[]{:S(2)}) collective-permute-start(bf16[64,2048]{1,0:T(8,128)(2,1)S(1)} %constant_dynamic-slice_fusion.3), channel_id=1, source_target_pairs={{0,16},{2,18},{4,20},{6,22},{8,24},{10,26},{12,28},{14,30},{16,0},... | collective-permute-start | bytes 786440 | tf_op jit(solution)/shard_map/ppermute | solution.py:200
  428.5 12.7 %collective-permute-start.8 = (bf16[128,1536]{1,0:T(8,128)(2,1)S(1)}, bf16[128,1536]{1,0:T(8,128)(2,1)S(1)}, u32[]{:S(2)}, u32[]{:S(2)}) collective-permute-start(bf16[128,1536]{1,0:T(8,128)(2,1)S(1)} %constant_dynamic-slice_fusion.11), channel_id=1, source_target_pairs={{0,8},{2,10},{4,12},{6,14},{8,0},{10,2},{12,4},{14,6},{16,24},{18,... | collective-permute-start | bytes 1179656 | tf_op jit(solution)/shard_map/ppermute | solution.py:200
  441.4 7.7 %collective-permute-start.9 = (bf16[64,1536]{1,0:T(8,128)(2,1)S(1)}, bf16[64,1536]{1,0:T(8,128)(2,1)S(1)}, u32[]{:S(2)}, u32[]{:S(2)}) collective-permute-start(bf16[64,1536]{1,0:T(8,128)(2,1)S(1)} %constant_dynamic-slice_fusion.10), channel_id=1, source_target_pairs={{0,16},{2,18},{4,20},{6,22},{8,24},{10,26},{12,28},{14,30},{16,0},... | collective-permute-start | bytes 589832 | tf_op jit(solution)/shard_map/ppermute | solution.py:200
  (62 other events, 690.3 us)
